TPU v7x, 32 devices: a whole 2x2x4 slice. The times are simulated.
32 devices in a mesh: seg: 8 (over y, x, core), row: 4 (over z).
Axes of the slice: x: 2, y: 2, z: 4, core: 2. Of those that a mesh axis runs over, the one named last changes fastest.
Arguments:
- left_env: bfloat16 [8, 512, 12, 512], P('seg', 'row'), may hold values from -4 to 4, as said below
- right_env: bfloat16 [8, 512, 12, 512], P('seg'), may hold values from -4 to 4, as said below
- site_operator: bfloat16 [4, 12, 12, 4], replicated, may hold values from -1 to 2, as said below
- start_vector: float32 [8, 512, 4, 512], P('seg', 'row'), may hold values from -6 to 6
Outputs:
- last_vector: float32 [8, 512, 4, 512], P('seg', 'row')
- alpha_values: float32 [8, 2], P('seg')
- beta_values: float32 [8, 2], P('seg')
Inputs may be any that keep to these rules, and one draw needn't show every extreme that they name: left_env[i, a, w, c] = left_env[i, c, w, a]. right_env[i, a, w, c] = right_env[i, c, w, a]. site_operator[s, v, w, r] = site_operator[r, v, w, s].
All inputs are finite; a program needn't handle non-finite values.
Results may differ from a plain program's by a relative error of at most 0.0076.
Values may be sent and summed in bfloat16 or wider, within the bound.
A program may use at most 128 MiB of HBM per device.

v0:
```python
import jax
import jax.numpy as jnp
from jax import lax
from jax.sharding import PartitionSpec as P

ITERS = 2


def passed_along(value, axis, steps):
    count = lax.axis_size(axis)
    initial, last = (max(0, -steps), min(count, count - steps))
    return lax.ppermute(value, axis, [(source, source + steps) for source in range(initial, last)])


def local(left_env, right_env, site_operator, start_vector):
    rows_here = left_env.shape[1]
    channels = left_env.shape[2]
    bond_width = left_env.shape[3]
    physical = site_operator.shape[0]
    entries = float(bond_width * physical * bond_width)
    left_local = left_env[0]
    operator_mat = site_operator.reshape(physical * channels, channels * physical)
    last_segment = lax.axis_index("seg") == lax.axis_size("seg") - 1
    received = passed_along(right_env, "seg", -1)
    right_used = jnp.where(last_segment, right_env, received)
    right_mat = right_used[0].reshape(bond_width, channels * bond_width)
    start_local = start_vector[0]
    norm_start = lax.psum(jnp.sum(start_local * start_local), "row") / entries
    current = start_local / jnp.sqrt(norm_start + 1e-06)
    previous = jnp.zeros_like(current)
    beta_prev = jnp.zeros((), jnp.float32)
    alpha_list = []
    beta_list = []
    for step_index in range(ITERS):
        lowered = current.astype(jnp.bfloat16)
        gathered = lax.all_gather(lowered, "row", axis=0, tiled=True)
        contracted = jnp.dot(
            left_local.reshape(rows_here * channels, bond_width),
            gathered.reshape(bond_width, physical * bond_width),
            preferred_element_type=jnp.float32,
        )
        contracted = contracted.astype(jnp.bfloat16).reshape(
            rows_here, channels * physical, bond_width
        )
        mixed = jnp.einsum(
            "ik,akb->aib", operator_mat, contracted, preferred_element_type=jnp.float32
        )
        mixed = mixed.astype(jnp.bfloat16).reshape(rows_here, physical, channels * bond_width)
        image = jnp.einsum("asc,bc->asb", mixed, right_mat, preferred_element_type=jnp.float32)
        image_image, image_curr, image_prev, curr_curr, prev_prev, curr_prev = lax.psum(
            (
                jnp.sum(image * image),
                jnp.sum(image * current),
                jnp.sum(image * previous),
                jnp.sum(current * current),
                jnp.sum(previous * previous),
                jnp.sum(current * previous),
            ),
            "row",
        )
        alpha = image_curr / entries
        norm_sq = (
            image_image
            - 2.0 * alpha * image_curr
            - 2.0 * beta_prev * image_prev
            + alpha * alpha * curr_curr
            + beta_prev * beta_prev * prev_prev
            + 2.0 * alpha * beta_prev * curr_prev
        ) / entries
        residual_vec = image - alpha * current - beta_prev * previous
        beta_next = jnp.sqrt(norm_sq + 1e-06)
        previous = current
        current = residual_vec / beta_next
        beta_prev = beta_next
        alpha_list.append(alpha)
        beta_list.append(beta_next)
    alpha_values = jnp.stack(alpha_list).reshape(1, ITERS)
    beta_values = jnp.stack(beta_list).reshape(1, ITERS)
    return (current[None], alpha_values, beta_values)


def solution(mesh):
    placed = (
        P("seg", "row", None, None),
        P("seg", None, None, None),
        P(),
        P("seg", "row", None, None),
    )
    return jax.shard_map(
        local,
        mesh=mesh,
        in_specs=placed,
        out_specs=(P("seg", "row", None, None), P("seg", None), P("seg", None)),
        check_vma=False,
    )
```

profile of v0, /device:TPU:0, one launch (start us, length us, event | category | flops | bytes accessed | tf_op | source)
XLA Modules:
  0.0 300.8 jit_solution(16806568525329012419)
XLA Ops:
  7.2 8.7 %copy.18 = bf16[1,512,12,512]{1,3,2,0:T(8,128)(2,1)} copy(bf16[1,512,12,512]{3,1,2,0:T(8,128)(2,1)} %param.5) | data formatting | bytes 12582912 | tf_op args[1]
  15.9 1.4 collective-permute-start
  17.4 1.1 multiply_reduce_fusion.5
  18.5 14.0 %psum.87 = f32[]{:T(128)} all-reduce(f32[]{:T(128)} %multiply_reduce_fusion.5), channel_id=1, replica_groups=mesh['seg'=8,'row'=4] {'row'}, use_global_device_ids=true, to_apply=%region_1.2 | all-reduce | flops 1 | bytes 8 | tf_op jit(solution)/shard_map/psum | solution.py:28
  33.2 1.1 bitcast_convert_fusion
  34.4 2.3 copy.13
  36.7 1.4 reshape_squeeze.7
  38.1 0.2 copy.15
  38.3 0.1 reshape.38
  38.4 41.6 %all-gather.3.cloned.1.call-done = bf16[512,4,512]{2,0,1:T(8,128)(2,1)} async-done(((bf16[128,4,512]{2,0,1:T(8,128)(2,1)}), bf16[512,4,512]{2,0,1:T(8,128)(2,1)}) %all-gather.3.cloned.1.call-update) | async-done | bytes 2097168 | tf_op jit(solution)/shard_map/all_gather | solution.py:36
  80.0 2.8 copy.12
  82.8 6.8 %fusion = bf16[1536,2048]{0,1:T(8,128)(2,1)} fusion(bf16[512,2048]{0,1:T(8,128)(2,1)S(1)} %bitcast.73, bf16[1536,512]{1,0:T(8,128)(2,1)} %reshape_squeeze.7), kind=kOutput, calls=%fused_computation.2 | convolution fusion | flops 3224371200 | bytes 9961472 | tf_op jit(solution)/shard_map/dot_general | solution.py:37
  89.6 8.6 %copy.14 = bf16[1536,2048]{1,0:T(8,128)(2,1)} copy(bf16[1536,2048]{0,1:T(8,128)(2,1)} %fusion) | data formatting | bytes 12582912 | tf_op jit(solution)/shard_map/convert_element_type | solution.py:42
  98.2 10.7 %reshape.37 = bf16[128,48,512]{2,1,0:T(8,128)(2,1)} reshape(bf16[1536,2048]{1,0:T(8,128)(2,1)} %copy.14) | data formatting | bytes 12582912 | tf_op jit(solution)/shard_map/reshape | solution.py:42
  108.9 7.3 %convert_bitcast_fusion.1 = bf16[128,48,512]{2,1,0:T(8,128)(2,1)} fusion(bf16[128,48,512]{2,1,0:T(8,128)(2,1)} %reshape.37, bf16[48,48]{0,1:T(8,128)(2,1)S(1)} %reshape.38), kind=kOutput, calls=%fused_computation.9 | convolution fusion | flops 305135616 | bytes 12587520 | tf_op jit(solution)/shard_map/ik,akb->aib/dot_general | solution.py:45
  116.2 13.6 %reshape.39 = bf16[128,4,6144]{2,1,0:T(4,128)(2,1)} reshape(bf16[128,48,512]{2,1,0:T(8,128)(2,1)} %convert_bitcast_fusion.1) | data formatting | bytes 12582912 | tf_op jit(solution)/shard_map/reshape | solution.py:48
  129.8 6.1 %broadcast_select_fusion = bf16[1,512,12,512]{1,3,2,0:T(8,128)(2,1)} fusion(bf16[1,512,12,512]{1,3,2,0:T(8,128)(2,1)} %copy.18, bf16[1,512,12,512]{1,3,2,0:T(8,128)(2,1)} %collective-permute-done, pred[]{:T(512)S(6)} %eq.3), kind=kLoop, calls=%fused_computation.10 | loop fusion | flops 3145728 | bytes 18874368 | tf_op jit(solution)/shard_map/jit(_where)/select_n | solution.py:25
  135.9 11.5 %fusion.10 = (f32[]{:T(128)}, f32[]{:T(128)}, f32[]{:T(128)}, f32[]{:T(128)}, f32[]{:T(128)}, /*index=5*/f32[128,4,512]{2,0,1:T(8,128)S(1)}) fusion(f32[]{:T(128)S(6)} %sqrt.9, f32[1,128,4,512]{3,2,1,0:T(4,128)S(1)} %copy-done, bf16[512,6144,1]{0,1,2:T(8,128)(2,1)} %bitcast.70, bf16[128,4,6144]{2,1,0:T(4,128)(2,1)} %reshape.39), kind=kOutput, calls=%fused_computation.23 | convolution fusion | flops 3224109056 | bytes 14680088 | tf_op jit(solution)/shard_map/asc,bc->asb/dot_general | solution.py:49
  147.4 10.9 %all-reduce.1 = (f32[]{:T(128)}, f32[]{:T(128)}, f32[]{:T(128)}, f32[]{:T(128)}, f32[]{:T(128)}, /*index=5*/f32[]{:T(128)}) all-reduce(f32[]{:T(128)} %get-tuple-element.18, f32[]{:T(128)} %get-tuple-element.16, f32[]{:T(128)} %get-tuple-element.17, f32[]{:T(128)} %get-tuple-element.15, ...), channel_id=1, replica_groups=mesh['seg'=8,'row'=4] {'row'}, use_global_device_ids=true, to_apply=%region_5.6 | all-reduce | flops 6 | bytes 48 | tf_op jit(solution)/shard_map/psum | solution.py:50
  165.4 1.2 fusion.18
  167.3 43.9 %all-gather.5.cloned.1.call-done = bf16[512,4,512]{2,0,1:T(8,128)(2,1)} async-done(((bf16[128,4,512]{2,0,1:T(8,128)(2,1)}), bf16[512,4,512]{2,0,1:T(8,128)(2,1)}) %all-gather.5.cloned.1.call-update) | async-done | bytes 2097168 | tf_op jit(solution)/shard_map/all_gather | solution.py:36
  211.2 4.2 %copy.21 = bf16[512,4,512]{0,2,1:T(8,128)(2,1)} copy(bf16[512,4,512]{2,0,1:T(8,128)(2,1)} %all-gather.5.cloned.1.call-done) | data formatting | bytes 4194304 | tf_op jit(solution)/shard_map/all_gather | solution.py:36
  215.3 8.2 %fusion.1 = bf16[1536,2048]{0,1:T(8,128)(2,1)} fusion(bf16[512,2048]{0,1:T(8,128)(2,1)} %bitcast.72, bf16[1536,512]{1,0:T(8,128)(2,1)} %reshape_squeeze.7), kind=kOutput, calls=%fused_computation.3 | convolution fusion | flops 3224371200 | bytes 9961472 | tf_op jit(solution)/shard_map/dot_general | solution.py:37
  223.5 8.6 %copy.22 = bf16[1536,2048]{1,0:T(8,128)(2,1)} copy(bf16[1536,2048]{0,1:T(8,128)(2,1)} %fusion.1) | data formatting | bytes 12582912 | tf_op jit(solution)/shard_map/convert_element_type | solution.py:42
  232.1 10.7 %reshape.41 = bf16[128,48,512]{2,1,0:T(8,128)(2,1)} reshape(bf16[1536,2048]{1,0:T(8,128)(2,1)} %copy.22) | data formatting | bytes 12582912 | tf_op jit(solution)/shard_map/reshape | solution.py:42
  242.8 7.2 %convert_bitcast_fusion = bf16[128,48,512]{2,1,0:T(8,128)(2,1)} fusion(bf16[128,48,512]{2,1,0:T(8,128)(2,1)} %reshape.41, bf16[48,48]{0,1:T(8,128)(2,1)S(1)} %reshape.38), kind=kOutput, calls=%fused_computation.8 | convolution fusion | flops 305135616 | bytes 12587520 | tf_op jit(solution)/shard_map/ik,akb->aib/dot_general | solution.py:45
  250.0 13.6 %reshape.42 = bf16[128,4,6144]{2,1,0:T(4,128)(2,1)} reshape(bf16[128,48,512]{2,1,0:T(8,128)(2,1)} %convert_bitcast_fusion) | data formatting | bytes 12582912 | tf_op jit(solution)/shard_map/reshape | solution.py:48
  263.6 11.5 %fusion.15 = (f32[]{:T(128)}, f32[]{:T(128)}, f32[]{:T(128)}, f32[]{:T(128)}, f32[]{:T(128)}, /*index=5*/f32[128,4,512]{2,0,1:T(8,128)S(1)}) fusion(f32[128,4,512]{2,0,1:T(8,128)S(1)} %get-tuple-element.31, f32[]{:T(128)S(6)} %sqrt.9, f32[1,128,4,512]{3,2,1,0:T(4,128)S(1)} %copy-done, bf16[512,6144,1]{0,1,2:T(8,128)(2,1)} %bitcast.71, ...), kind=kOutput, calls=%fused_computation.28 | convolution fusion | flops 3224109056 | bytes 15728664 | tf_op jit(solution)/shard_map/asc,bc->asb/dot_general | solution.py:49
  275.1 10.2 %all-reduce = (f32[]{:T(128)}, f32[]{:T(128)}, f32[]{:T(128)}, f32[]{:T(128)}, f32[]{:T(128)}) all-reduce(f32[]{:T(128)} %get-tuple-element.12, f32[]{:T(128)} %get-tuple-element.11, f32[]{:T(128)} %get-tuple-element.10, f32[]{:T(128)} %get-tuple-element.13, f32[]{:T(128)} %get-tuple-element.9), channel_id=1, replica_groups=mesh['seg'=8,'row'=4] {'row'}, use_global_device_ids=true, to_apply=%region_16.17 | all-reduce | flops 5 | bytes 40 | tf_op jit(solution)/shard_map/psum | solution.py:50
  291.2 0.5 fusion.13
  291.7 1.6 copy.26
  293.3 0.6 maximum_bitcast_fusion
  (9 shorter events, 0.1 us)
Async XLA Ops:
  7.2 10.2 %copy-start = (f32[1,128,4,512]{3,2,1,0:T(4,128)S(1)}, f32[1,128,4,512]{3,2,1,0:T(4,128)}, u32[]{:S(2)}) copy-start(f32[1,128,4,512]{3,2,1,0:T(4,128)} %param.7) | copy-start | bytes 3145732
  7.2 72.9 %all-gather.3.cloned.1.call-start = ((), (), s32[]{:S(2)}) async-start(), calls=%async_computation | async-start | bytes 2621440 | tf_op jit(solution)/shard_map/all_gather | solution.py:36
  15.9 22.1 %copy-start.1 = (bf16[4,12,12,4]{2,3,1,0:T(4,128)(2,1)S(1)}, bf16[4,12,12,4]{2,3,1,0:T(4,128)(2,1)}, u32[]{:S(2)}) copy-start(bf16[4,12,12,4]{2,3,1,0:T(4,128)(2,1)} %param.6) | copy-start | bytes 13828
  15.9 113.9 %collective-permute-start = (bf16[1,512,12,512]{1,3,2,0:T(8,128)(2,1)}, bf16[1,512,12,512]{1,3,2,0:T(8,128)(2,1)}, u32[]{:S(2)}, u32[]{:S(2)}) collective-permute-start(bf16[1,512,12,512]{1,3,2,0:T(8,128)(2,1)} %copy.18), channel_id=1, source_target_pairs={{4,0},{8,4},{12,8},{16,12},{20,16},{24,20},{28,24},{5,1},{9,5},{13... | collective-permute-start | bytes 18874376 | tf_op jit(solution)/shard_map/ppermute | solution.py:12
  34.3 176.8 %all-gather.5.cloned.1.call-start = ((), (), s32[]{:S(2)}) async-start(), calls=%async_computation.1 | async-start | bytes 2621440 | tf_op jit(solution)/shard_map/all_gather | solution.py:36
Sparse Core Ops, SparseCore 0:
  34.4 45.5 all-gather.2
  166.7 44.3 all-gather.4
where the time goes:
time: 303 us; the launch traced here: 301 us
  local copies, waits for them, and re-layouts  87.1 us (29%)
  waiting for transfers between devices  85.5 us (28%)
  matrix products  52.4 us (17%)
  blocking collectives  35.1 us (12%)
  between operations  28.4 us (9%)
  other arithmetic  10.6 us (3%)
    all_gather x2, waiting for transfers between devices, local(): gathered = lax.all_gather(lowered, 'row', axis=0, tiled=True)  85.5 us
    reshape x2, local copies, waits for them, and re-layouts, local(): mixed.astype(jnp.bfloat16)  27.2 us
    dot_general x2, matrix products, local(): jnp.einsum('asc,bc->asb', mixed, right_mat, preferred_element_type=jnp.fl...  22.9 us
    reshape x2, local copies, waits for them, and re-layouts, local(): contracted.astype(jnp.bfloat16)  21.4 us
    psum x2, blocking collectives, local(): lax.psum((jnp.sum(image * image), jnp.sum(image * current), jnp.sum(image...  21.1 us
    convert_element_type x2, local copies, waits for them, and re-layouts, local(): contracted.astype(jnp.bfloat16)  17.2 us
    dot_general x2, matrix products, local(): jnp.dot(left_local.reshape(rows_here * channels, bond_width), gathered.re...  14.9 us
    dot_general x2, matrix products, local(): jnp.einsum('ik,akb->aib', operator_mat, contracted, preferred_element_typ...  14.6 us
  transfers between devices with their start and end apart: 3, of which 2 were waited for; matrix products, arithmetic and copies ran while one was open for 19% of the time, Pallas kernels for 0%

commit v1 on v0

--- a/solution.py
+++ b/solution.py
@@ -33,7 +33,25 @@
     beta_list = []
     for step_index in range(ITERS):
         lowered = current.astype(jnp.bfloat16)
-        gathered = lax.all_gather(lowered, "row", axis=0, tiled=True)
+        ways, here, step = (lax.axis_size("row"), lax.axis_index("row"), lowered.shape[0])
+        shape = [n * ways if d == 0 else n for d, n in enumerate(lowered.shape)]
+        full = lax.dynamic_update_slice_in_dim(
+            jnp.zeros(shape, lowered.dtype), lowered, here * step, axis=0
+        )
+        going_up = going_down = lowered
+        for far in range(1, ways // 2 + 1):
+            going_up = lax.ppermute(going_up, "row", [(d, (d + 1) % ways) for d in range(ways)])
+            full = lax.dynamic_update_slice_in_dim(
+                full, going_up, (here - far) % ways * step, axis=0
+            )
+            if 2 * far < ways:
+                going_down = lax.ppermute(
+                    going_down, "row", [(d, (d - 1) % ways) for d in range(ways)]
+                )
+                full = lax.dynamic_update_slice_in_dim(
+                    full, going_down, (here + far) % ways * step, axis=0
+                )
+        gathered = full
         contracted = jnp.dot(
             left_local.reshape(rows_here * channels, bond_width),
             gathered.reshape(bond_width, physical * bond_width),

time: 303 us -> 274 us (0.904); the launches traced: 301 us -> 268 us
  waiting for transfers between devices: 85.5 us -> 41.2 us
  local copies, waits for them, and re-layouts: 87.1 us -> 102 us
  between operations: 28.4 us -> 14.8 us
  starting transfers between devices: 1.49 us -> 11.9 us
    all_gather x2 -> x0, waiting for transfers between devices: 85.5 us -> none  [local(): gathered = lax.all_gather(lowered, 'row', axis=0, tiled=True)]
    ppermute x0 -> x6, waiting for transfers between devices: none -> 41.2 us  [the longest x4 39.4 us: local(): lax.ppermute(going_up, 'row', [(d, (d + 1) % ways) for d in range(ways)])]
    ppermute x0 -> x6, starting transfers between devices: none -> 10.5 us  [the longest x2 5.68 us: local(): lax.ppermute(going_down, 'row', [(d, (d - 1) % ways) for d in range(ways)])]
    ppermute x0 -> x6, local copies, waits for them, and re-layouts: none -> 10 us  [the longest x4 6.7 us: local(): lax.ppermute(going_up, 'row', [(d, (d + 1) % ways) for d in range(ways)])]
    dynamic_update_slice x0 -> x8, local copies, waits for them, and re-layouts: none -> 8.16 us  [the longest x4 4.09 us: local(): lax.dynamic_update_slice_in_dim(full, going_up, (here - far) % ways * ste...]
    all_gather x2 -> x0, local copies, waits for them, and re-layouts: 6.95 us -> none  [local(): gathered = lax.all_gather(lowered, 'row', axis=0, tiled=True)]
  transfers between devices with their start and end apart: 3 -> 7, of which waited for: 2 -> 5; matrix products, arithmetic and copies ran while one was open for 19% -> 27% of each run, Pallas kernels for 0% -> 0%
where the time goes in v1:
time: 274 us; the launch traced here: 268 us
  local copies, waits for them, and re-layouts  102 us (37%)
  matrix products  54.4 us (20%)
  waiting for transfers between devices  41.2 us (15%)
  blocking collectives  32.7 us (12%)
  between operations  14.8 us (5%)
  starting transfers between devices  11.9 us (4%)
  other arithmetic  11 us (4%)
    ppermute x4, waiting for transfers between devices, local(): lax.ppermute(going_up, 'row', [(d, (d + 1) % ways) for d in range(ways)])  39.4 us
    reshape x2, local copies, waits for them, and re-layouts, local(): mixed.astype(jnp.bfloat16)  27.2 us
    dot_general x2, matrix products, local(): jnp.einsum('asc,bc->asb', mixed, right_mat, preferred_element_type=jnp.fl...  24.9 us
    reshape x2, local copies, waits for them, and re-layouts, local(): contracted.astype(jnp.bfloat16)  21.4 us
    psum x2, blocking collectives, local(): lax.psum((jnp.sum(image * image), jnp.sum(image * current), jnp.sum(image...  18.7 us
    convert_element_type x2, local copies, waits for them, and re-layouts, local(): contracted.astype(jnp.bfloat16)  17.2 us
    dot_general x2, matrix products, local(): jnp.dot(left_local.reshape(rows_here * channels, bond_width), gathered.re...  14.9 us
    dot_general x2, matrix products, local(): jnp.einsum('ik,akb->aib', operator_mat, contracted, preferred_element_typ...  14.6 us
  transfers between devices with their start and end apart: 7, of which 5 were waited for; matrix products, arithmetic and copies ran while one was open for 27% of the time, Pallas kernels for 0%

profile of v1, /device:TPU:0, one launch (start us, length us, event | category | flops | bytes accessed | tf_op | source)
XLA Modules:
  0.0 268.4 jit_solution(9812573151616192616)
XLA Ops:
  0.6 8.7 %copy.21 = bf16[1,512,12,512]{1,3,2,0:T(8,128)(2,1)} copy(bf16[1,512,12,512]{3,1,2,0:T(8,128)(2,1)} %param.5) | data formatting | bytes 12582912 | tf_op args[1]
  11.9 14.0 %psum.87 = f32[]{:T(128)} all-reduce(f32[]{:T(128)} %multiply_reduce_fusion.5), channel_id=1, replica_groups=mesh['seg'=8,'row'=4] {'row'}, use_global_device_ids=true, to_apply=%region_1.2 | all-reduce | flops 1 | bytes 8 | tf_op jit(solution)/shard_map/psum | solution.py:28
  27.7 3.8 %collective-permute-start.1 = (bf16[128,4,512]{2,0,1:T(8,128)(2,1)}, bf16[128,4,512]{2,0,1:T(8,128)(2,1)}, u32[]{:S(2)}, u32[]{:S(2)}) collective-permute-start(bf16[128,4,512]{2,0,1:T(8,128)(2,1)} %bitcast_convert_fusion), channel_id=1, source_target_pairs={{0,3},{1,0},{2,1},{3,2},{4,7},{5,4},{6,5},{7,6},{8,11},{9,8},{10,9... | collective-permute-start | bytes 1572872 | tf_op jit(solution)/shard_map/ppermute | solution.py:48
  31.6 13.2 %collective-permute-done = bf16[128,4,512]{2,0,1:T(8,128)(2,1)} collective-permute-done((bf16[128,4,512]{2,0,1:T(8,128)(2,1)}, bf16[128,4,512]{2,0,1:T(8,128)(2,1)}, u32[]{:S(2)}, u32[]{:S(2)}) %collective-permute-start) | collective-permute-done | bytes 524320 | tf_op jit(solution)/shard_map/ppermute | solution.py:43
  44.7 2.0 copy.12
  46.8 2.3 copy.16
  52.1 2.0 copy.13
  54.2 2.0 copy.14
  58.6 6.9 %collective-permute-done.2 = bf16[128,4,512]{2,0,1:T(8,128)(2,1)} collective-permute-done((bf16[128,4,512]{2,0,1:T(8,128)(2,1)}, bf16[128,4,512]{2,0,1:T(8,128)(2,1)}, u32[]{:S(2)}, u32[]{:S(2)}) %collective-permute-start.2) | collective-permute-done | bytes 524320 | tf_op jit(solution)/shard_map/ppermute | solution.py:43
  65.4 2.0 copy.15
  68.6 6.7 %fusion = bf16[1536,2048]{0,1:T(8,128)(2,1)} fusion(bf16[512,2048]{0,1:T(8,128)(2,1)S(1)} %bitcast.72, bf16[1536,512]{1,0:T(8,128)(2,1)} %reshape_squeeze.7), kind=kOutput, calls=%fused_computation.2 | convolution fusion | flops 3224371200 | bytes 9961472 | tf_op jit(solution)/shard_map/dot_general | solution.py:55
  75.4 8.6 %copy.17 = bf16[1536,2048]{1,0:T(8,128)(2,1)} copy(bf16[1536,2048]{0,1:T(8,128)(2,1)} %fusion) | data formatting | bytes 12582912 | tf_op jit(solution)/shard_map/convert_element_type | solution.py:60
  84.0 10.7 %reshape.37 = bf16[128,48,512]{2,1,0:T(8,128)(2,1)} reshape(bf16[1536,2048]{1,0:T(8,128)(2,1)} %copy.17) | data formatting | bytes 12582912 | tf_op jit(solution)/shard_map/reshape | solution.py:60
  94.7 7.3 %convert_bitcast_fusion.1 = bf16[128,48,512]{2,1,0:T(8,128)(2,1)} fusion(bf16[128,48,512]{2,1,0:T(8,128)(2,1)} %reshape.37, bf16[48,48]{0,1:T(8,128)(2,1)S(1)} %reshape.38), kind=kOutput, calls=%fused_computation.9 | convolution fusion | flops 305135616 | bytes 12587520 | tf_op jit(solution)/shard_map/ik,akb->aib/dot_general | solution.py:63
  102.0 13.6 %reshape.39 = bf16[128,4,6144]{2,1,0:T(4,128)(2,1)} reshape(bf16[128,48,512]{2,1,0:T(8,128)(2,1)} %convert_bitcast_fusion.1) | data formatting | bytes 12582912 | tf_op jit(solution)/shard_map/reshape | solution.py:66
  115.6 6.1 %broadcast_select_fusion = bf16[1,512,12,512]{1,3,2,0:T(8,128)(2,1)} fusion(bf16[1,512,12,512]{1,3,2,0:T(8,128)(2,1)} %copy.21, bf16[1,512,12,512]{1,3,2,0:T(8,128)(2,1)} %collective-permute-done.3, pred[]{:T(512)S(6)} %eq.10), kind=kLoop, calls=%fused_computation.10 | loop fusion | flops 3145728 | bytes 18874368 | tf_op jit(solution)/shard_map/jit(_where)/select_n | solution.py:25
  121.7 13.5 %fusion.10 = (f32[]{:T(128)}, f32[]{:T(128)}, f32[]{:T(128)}, f32[]{:T(128)}, f32[]{:T(128)}, /*index=5*/f32[128,4,512]{2,0,1:T(8,128)}) fusion(f32[]{:T(128)S(6)} %sqrt.9, f32[1,128,4,512]{3,2,1,0:T(4,128)S(1)} %copy-done, bf16[512,6144,1]{0,1,2:T(8,128)(2,1)} %bitcast.70, bf16[128,4,6144]{2,1,0:T(4,128)(2,1)} %reshape.39), kind=kOutput, calls=%fused_computation.23 | convolution fusion | flops 3224109056 | bytes 14680088 | tf_op jit(solution)/shard_map/asc,bc->asb/dot_general | solution.py:67
  135.2 9.6 %all-reduce.1 = (f32[]{:T(128)}, f32[]{:T(128)}, f32[]{:T(128)}, f32[]{:T(128)}, f32[]{:T(128)}, /*index=5*/f32[]{:T(128)}) all-reduce(f32[]{:T(128)} %get-tuple-element.18, f32[]{:T(128)} %get-tuple-element.16, f32[]{:T(128)} %get-tuple-element.17, f32[]{:T(128)} %get-tuple-element.15, ...), channel_id=1, replica_groups=mesh['seg'=8,'row'=4] {'row'}, use_global_device_ids=true, to_apply=%region_5.6 | all-reduce | flops 6 | bytes 48 | tf_op jit(solution)/shard_map/psum | solution.py:68
  153.2 2.0 collective-permute-start.4
  155.2 1.9 collective-permute-start.5
  157.1 12.9 %collective-permute-done.4 = bf16[128,4,512]{2,0,1:T(8,128)(2,1)} collective-permute-done((bf16[128,4,512]{2,0,1:T(8,128)(2,1)S(1)}, bf16[128,4,512]{2,0,1:T(8,128)(2,1)}, u32[]{:S(2)}, u32[]{:S(2)}) %collective-permute-start.4) | collective-permute-done | bytes 524320 | tf_op jit(solution)/shard_map/ppermute | solution.py:43
  170.0 2.8 %collective-permute-start.6 = (bf16[128,4,512]{2,0,1:T(8,128)(2,1)}, bf16[128,4,512]{2,0,1:T(8,128)(2,1)}, u32[]{:S(2)}, u32[]{:S(2)}) collective-permute-start(bf16[128,4,512]{2,0,1:T(8,128)(2,1)} %collective-permute-done.4), channel_id=1, source_target_pairs={{0,1},{1,2},{2,3},{3,0},{4,5},{5,6},{6,7},{7,4},{8,9},{9,10},{10,1... | collective-permute-start | bytes 1572872 | tf_op jit(solution)/shard_map/ppermute | solution.py:43
  177.4 1.8 collective-permute-done.5
  182.3 6.4 %collective-permute-done.6 = bf16[128,4,512]{2,0,1:T(8,128)(2,1)} collective-permute-done((bf16[128,4,512]{2,0,1:T(8,128)(2,1)}, bf16[128,4,512]{2,0,1:T(8,128)(2,1)}, u32[]{:S(2)}, u32[]{:S(2)}) %collective-permute-start.6) | collective-permute-done | bytes 524320 | tf_op jit(solution)/shard_map/ppermute | solution.py:43
  190.9 8.2 %fusion.1 = bf16[1536,2048]{0,1:T(8,128)(2,1)} fusion(bf16[512,2048]{0,1:T(8,128)(2,1)} %bitcast.7, bf16[1536,512]{1,0:T(8,128)(2,1)} %reshape_squeeze.7), kind=kOutput, calls=%fused_computation.3 | convolution fusion | flops 3224371200 | bytes 9961472 | tf_op jit(solution)/shard_map/dot_general | solution.py:55
  199.1 8.6 %copy.28 = bf16[1536,2048]{1,0:T(8,128)(2,1)} copy(bf16[1536,2048]{0,1:T(8,128)(2,1)} %fusion.1) | data formatting | bytes 12582912 | tf_op jit(solution)/shard_map/convert_element_type | solution.py:60
  207.7 10.7 %reshape.41 = bf16[128,48,512]{2,1,0:T(8,128)(2,1)} reshape(bf16[1536,2048]{1,0:T(8,128)(2,1)} %copy.28) | data formatting | bytes 12582912 | tf_op jit(solution)/shard_map/reshape | solution.py:60
  218.4 7.2 %convert_bitcast_fusion = bf16[128,48,512]{2,1,0:T(8,128)(2,1)} fusion(bf16[128,48,512]{2,1,0:T(8,128)(2,1)} %reshape.41, bf16[48,48]{0,1:T(8,128)(2,1)S(1)} %reshape.38), kind=kOutput, calls=%fused_computation.8 | convolution fusion | flops 305135616 | bytes 12587520 | tf_op jit(solution)/shard_map/ik,akb->aib/dot_general | solution.py:63
  225.7 13.6 %reshape.42 = bf16[128,4,6144]{2,1,0:T(4,128)(2,1)} reshape(bf16[128,48,512]{2,1,0:T(8,128)(2,1)} %convert_bitcast_fusion) | data formatting | bytes 12582912 | tf_op jit(solution)/shard_map/reshape | solution.py:66
  239.2 11.5 %fusion.15 = (f32[]{:T(128)}, f32[]{:T(128)}, f32[]{:T(128)}, f32[]{:T(128)}, f32[]{:T(128)}, /*index=5*/f32[128,4,512]{2,0,1:T(8,128)S(1)}) fusion(f32[128,4,512]{2,0,1:T(8,128)S(1)} %get-tuple-element.31, f32[]{:T(128)S(6)} %sqrt.9, f32[1,128,4,512]{3,2,1,0:T(4,128)S(1)} %copy-done, bf16[512,6144,1]{0,1,2:T(8,128)(2,1)} %bitcast.71, ...), kind=kOutput, calls=%fused_computation.28 | convolution fusion | flops 3224109056 | bytes 15728664 | tf_op jit(solution)/shard_map/asc,bc->asb/dot_general | solution.py:67
  250.7 9.1 %all-reduce = (f32[]{:T(128)}, f32[]{:T(128)}, f32[]{:T(128)}, f32[]{:T(128)}, f32[]{:T(128)}) all-reduce(f32[]{:T(128)} %get-tuple-element.12, f32[]{:T(128)} %get-tuple-element.11, f32[]{:T(128)} %get-tuple-element.10, f32[]{:T(128)} %get-tuple-element.13, f32[]{:T(128)} %get-tuple-element.9), channel_id=1, replica_groups=mesh['seg'=8,'row'=4] {'row'}, use_global_device_ids=true, to_apply=%region_16.17 | all-reduce | flops 5 | bytes 40 | tf_op jit(solution)/shard_map/psum | solution.py:68
  266.2 1.6 copy.32
  (31 shorter events, 22.1 us)
Async XLA Ops:
  0.6 10.2 %copy-start = (f32[1,128,4,512]{3,2,1,0:T(4,128)S(1)}, f32[1,128,4,512]{3,2,1,0:T(4,128)}, u32[]{:S(2)}) copy-start(f32[1,128,4,512]{3,2,1,0:T(4,128)} %param.7) | copy-start | bytes 3145732
  9.4 41.1 %copy-start.1 = (bf16[4,12,12,4]{2,3,1,0:T(4,128)(2,1)S(1)}, bf16[4,12,12,4]{2,3,1,0:T(4,128)(2,1)}, u32[]{:S(2)}) copy-start(bf16[4,12,12,4]{2,3,1,0:T(4,128)(2,1)} %param.6) | copy-start | bytes 13828
  9.4 106.3 %collective-permute-start.3 = (bf16[1,512,12,512]{1,3,2,0:T(8,128)(2,1)}, bf16[1,512,12,512]{1,3,2,0:T(8,128)(2,1)}, u32[]{:S(2)}, u32[]{:S(2)}) collective-permute-start(bf16[1,512,12,512]{1,3,2,0:T(8,128)(2,1)} %copy.21), channel_id=1, source_target_pairs={{4,0},{8,4},{12,8},{16,12},{20,16},{24,20},{28,24},{5,1},{9,5},{13... | collective-permute-start | bytes 18874376 | tf_op jit(solution)/shard_map/ppermute | solution.py:12
  27.7 17.0 %collective-permute-start = (bf16[128,4,512]{2,0,1:T(8,128)(2,1)}, bf16[128,4,512]{2,0,1:T(8,128)(2,1)}, u32[]{:S(2)}, u32[]{:S(2)}) collective-permute-start(bf16[128,4,512]{2,0,1:T(8,128)(2,1)} %bitcast_convert_fusion), channel_id=1, source_target_pairs={{0,1},{1,2},{2,3},{3,0},{4,5},{5,6},{6,7},{7,4},{8,9},{9,10},{10,1... | collective-permute-start | bytes 1572872 | tf_op jit(solution)/shard_map/ppermute | solution.py:43
  27.7 26.4 %collective-permute-start.1 = (bf16[128,4,512]{2,0,1:T(8,128)(2,1)}, bf16[128,4,512]{2,0,1:T(8,128)(2,1)}, u32[]{:S(2)}, u32[]{:S(2)}) collective-permute-start(bf16[128,4,512]{2,0,1:T(8,128)(2,1)} %bitcast_convert_fusion), channel_id=1, source_target_pairs={{0,3},{1,0},{2,1},{3,2},{4,7},{5,4},{6,5},{7,6},{8,11},{9,8},{10,9... | collective-permute-start | bytes 1572872 | tf_op jit(solution)/shard_map/ppermute | solution.py:48
  44.7 20.7 %collective-permute-start.2 = (bf16[128,4,512]{2,0,1:T(8,128)(2,1)}, bf16[128,4,512]{2,0,1:T(8,128)(2,1)}, u32[]{:S(2)}, u32[]{:S(2)}) collective-permute-start(bf16[128,4,512]{2,0,1:T(8,128)(2,1)} %collective-permute-done), channel_id=1, source_target_pairs={{0,1},{1,2},{2,3},{3,0},{4,5},{5,6},{6,7},{7,4},{8,9},{9,10},{10,1... | collective-permute-start | bytes 1572872 | tf_op jit(solution)/shard_map/ppermute | solution.py:43
  153.2 16.8 %collective-permute-start.4 = (bf16[128,4,512]{2,0,1:T(8,128)(2,1)S(1)}, bf16[128,4,512]{2,0,1:T(8,128)(2,1)}, u32[]{:S(2)}, u32[]{:S(2)}) collective-permute-start(bf16[128,4,512]{2,0,1:T(8,128)(2,1)S(1)} %get-tuple-element.30), channel_id=1, source_target_pairs={{0,1},{1,2},{2,3},{3,0},{4,5},{5,6},{6,7},{7,4},{8,9},{9,10},{10,1... | collective-permute-start | bytes 1572872 | tf_op jit(solution)/shard_map/ppermute | solution.py:43
  155.2 24.0 %collective-permute-start.5 = (bf16[128,4,512]{2,0,1:T(8,128)(2,1)S(1)}, bf16[128,4,512]{2,0,1:T(8,128)(2,1)}, u32[]{:S(2)}, u32[]{:S(2)}) collective-permute-start(bf16[128,4,512]{2,0,1:T(8,128)(2,1)S(1)} %get-tuple-element.30), channel_id=1, source_target_pairs={{0,3},{1,0},{2,1},{3,2},{4,7},{5,4},{6,5},{7,6},{8,11},{9,8},{10,9... | collective-permute-start | bytes 1572872 | tf_op jit(solution)/shard_map/ppermute | solution.py:48
  170.0 18.7 %collective-permute-start.6 = (bf16[128,4,512]{2,0,1:T(8,128)(2,1)}, bf16[128,4,512]{2,0,1:T(8,128)(2,1)}, u32[]{:S(2)}, u32[]{:S(2)}) collective-permute-start(bf16[128,4,512]{2,0,1:T(8,128)(2,1)} %collective-permute-done.4), channel_id=1, source_target_pairs={{0,1},{1,2},{2,3},{3,0},{4,5},{5,6},{6,7},{7,4},{8,9},{9,10},{10,1... | collective-permute-start | bytes 1572872 | tf_op jit(solution)/shard_map/ppermute | solution.py:43
